TPU v7x, 32 devices: a whole 2x2x4 slice. The times are simulated.
32 devices in a mesh: pts: 8 (over y, x, core), lmk: 4 (over z).
Axes of the slice: x: 2, y: 2, z: 4, core: 2. Of those that a mesh axis runs over, the one named last changes fastest.
Arguments:
- points: bfloat16 [2048, 768], P('pts'), may hold values from -6 to 6
- landmarks: bfloat16 [384, 768], P('lmk'), may hold values from -6 to 6
- panels: bfloat16 [8, 384, 2048], P('pts', None, 'lmk'), may hold values from -0.3125 to 0.3125
- panel_index: int32 [1], replicated, may hold values from 0 to 7
- assignment: int32 [2048], P('pts'), may hold values from 0 to 4095, as said below
Outputs:
- centroid_sums: float32 [4096, 2048], P('pts', 'lmk')
- cluster_counts: int32 [4096], P('pts')
Inputs may be any that keep to these rules, and one draw needn't show every extreme that they name: `assignment`: owner of a cluster c is c // 512. In each aligned block of 256 points (the points of one device) at most 64 points have clusters of one owner; one owner, the same for every block, has exactly 64 points in every block.
All inputs are finite; a program needn't handle non-finite values.
Results may differ from a plain program's by a relative error of at most 0.0017.
Values may be sent and summed in bfloat16 or wider, within the bound.
No kernel may reach another device: no remote copies, remote signals or barrier semaphores. Data moves between devices by JAX's collectives and lax.ppermute only.
A program may use at most 64 MiB of HBM per device.

v0:
```python
import math

import jax
import jax.numpy as jnp
from jax import lax
from jax.sharding import PartitionSpec as P

CLUSTERS = 4096


def spread(block, axis, holder):
    block = jnp.where(lax.axis_index(axis) == holder, block, jnp.zeros_like(block))
    return lax.psum(block, axis)


def unit_rows(values_in):
    widened = values_in.astype(jnp.float32)
    scale = lax.rsqrt(jnp.mean(widened * widened, axis=1, keepdims=True) + 1e-06)
    return (widened * scale).astype(jnp.bfloat16)


def kernel_rows(unit_points, unit_marks):
    scores = lax.dot_general(
        unit_points, unit_marks, (((1,), (1,)), ((), ())), preferred_element_type=jnp.float32
    )
    return jnp.exp(scores * (0.5 / math.sqrt(unit_points.shape[1]))).astype(jnp.bfloat16)


def body(points, landmarks, panels, panel_index, assignment):
    point_groups = lax.axis_size("pts")
    point_rows = points.shape[0]
    unit_points = unit_rows(points)
    kernel = kernel_rows(
        unit_points, unit_rows(lax.all_gather(landmarks, "lmk", axis=0, tiled=True))
    )
    factor_panel = spread(panels[0], "pts", panel_index[0])
    owned_clusters = CLUSTERS // point_groups
    capacity = 2 * point_rows // point_groups
    owners = assignment // owned_clusters
    local_id = assignment - owners * owned_clusters
    owner_hits = (owners[:, None] == jnp.arange(point_groups, dtype=jnp.int32)[None, :]).astype(
        jnp.int32
    )
    slot_rank = jnp.sum(jnp.cumsum(owner_hits, axis=0) * owner_hits, axis=1) - 1
    slot_ids = jnp.full((point_groups, capacity), -1, jnp.int32).at[owners, slot_rank].set(local_id)
    features = jnp.dot(kernel, factor_panel, preferred_element_type=jnp.float32).astype(
        jnp.bfloat16
    )
    slots = (
        jnp.zeros((point_groups, capacity, features.shape[1]), jnp.bfloat16)
        .at[owners, slot_rank]
        .set(features)
    )
    arrived, arrived_ids = (
        lax.all_to_all(slots, "pts", split_axis=0, concat_axis=0, tiled=True),
        lax.all_to_all(slot_ids, "pts", split_axis=0, concat_axis=0, tiled=True),
    )
    received = arrived.reshape(-1, arrived.shape[2])
    membership = (
        arrived_ids.reshape(-1)[None, :] == jnp.arange(owned_clusters, dtype=jnp.int32)[:, None]
    )
    totals = jnp.dot(membership.astype(jnp.bfloat16), received, preferred_element_type=jnp.float32)
    counts = jnp.sum(membership.astype(jnp.int32), axis=1)
    mean_count = point_rows * point_groups / CLUSTERS
    return (totals / mean_count, counts)


def solution(mesh):
    in_specs = (P("pts", None), P("lmk", None), P("pts", None, "lmk"), P(), P("pts"))
    out_specs = (P("pts", "lmk"), P("pts"))
    return jax.shard_map(body, mesh=mesh, in_specs=in_specs, out_specs=out_specs, check_vma=False)
```

profile of v0, /device:TPU:0, one launch (start us, length us, event | category | flops | bytes accessed | tf_op | source)
XLA Modules:
  0.0 129.5 jit_solution(13763068009029808831)
XLA Ops:
  7.2 0.0 all-reduce.2.cloned.1.call-start
  7.9 0.8 select_bitcast_fusion
  8.7 0.0 all-reduce.2.cloned.1.call-update
  8.7 0.6 reduce-window.6
  9.3 0.2 slice_reduce_fusion
  9.6 0.1 fusion.16
  9.7 0.6 broadcast_in_dim.8
  10.3 38.3 %scatter_fusion = s32[8,64]{1,0:T(8,128)} fusion(s32[8,64]{1,0:T(8,128)} %broadcast_in_dim.8, s32[256]{0:T(256)S(1)} %bitcast.21, s32[256]{0:T(256)S(1)} %get-tuple-element.2), kind=kCustom, calls=%fused_computation | custom fusion | bytes 5120 | tf_op jit(solution)/shard_map/scatter | solution.py:45
  48.6 5.4 %all-to-all-start = ((s32[8,1,64]{2,1,0:T(1,128)}), s32[8,1,64]{2,1,0:T(1,128)S(1)}, u32[]{:S(2)}, u32[]{:S(2)}) async-start(s32[8,1,64]{2,1,0:T(1,128)} %bitcast.8), calls=%async_computation | async-start | bytes 8192 | tf_op jit(solution)/shard_map/all_to_all | solution.py:56
  54.0 17.6 %all_gather.3 = bf16[384,768]{1,0:T(8,128)(2,1)S(1)} all-gather(bf16[96,768]{1,0:T(8,128)(2,1)S(1)} %copy-done.1), channel_id=1, replica_groups=mesh['pts'=8,'lmk'=4] {'lmk'}, dimensions={0}, use_global_device_ids=true | all-gather | bytes 737280 | tf_op jit(solution)/shard_map/all_gather | solution.py:34
  71.6 0.2 fusion.1
  71.8 0.2 fusion.4
  72.0 0.0 all-reduce.2.cloned.1.call-done
  72.0 1.7 %convolution_convert_fusion = bf16[256,512]{1,0:T(8,128)(2,1)S(1)} fusion(bf16[384,512]{1,0:T(8,128)(2,1)} %all-reduce.2.cloned.1.call-done, bf16[384,768]{1,0:T(8,128)(2,1)S(1)} %all_gather.3, f32[384]{0:T(512)S(1)} %add_rsqrt_fusion, bf16[256,768]{1,0:T(8,128)(2,1)S(1)} %copy-done, f32[256]{0:T(256)S(1)} %add_rsqrt_fusion.1), kind=kOutput, calls=%fused_computation.5 | convolution fusion | flops 253460480 | bytes 1640960 | tf_op jit(solution)/shard_map/dot_general | solution.py:46
  73.7 0.8 broadcast_in_dim.10
  74.6 33.0 %scatter_fusion.1 = bf16[8,64,512]{2,1,0:T(8,128)(2,1)} fusion(bf16[8,64,512]{2,1,0:T(8,128)(2,1)} %broadcast_in_dim.10, s32[256]{0:T(256)S(1)} %bitcast.22, bf16[256,512]{1,0:T(8,128)(2,1)S(1)} %convolution_convert_fusion), kind=kCustom, calls=%fused_computation.1 | custom fusion | bytes 788480 | tf_op jit(solution)/shard_map/scatter | solution.py:52
  107.6 0.0 all-to-all-done
  107.6 3.9 %all-to-all-start.1 = ((bf16[8,64,512]{2,1,0:T(8,128)(2,1)}), bf16[8,64,512]{2,1,0:T(8,128)(2,1)S(1)}, u32[]{:S(2)}, u32[]{:S(2)}) async-start(bf16[8,64,512]{2,1,0:T(8,128)(2,1)} %scatter_fusion.1), calls=%async_computation.1 | async-start | bytes 1048576 | tf_op jit(solution)/shard_map/all_to_all | solution.py:55
  111.5 0.5 broadcast.136
  112.0 0.7 reduce.5
  112.7 0.1 eq.48
  112.7 0.8 convert_reduce_fusion
  113.5 7.7 %all-to-all-done.1 = bf16[8,64,512]{2,1,0:T(8,128)(2,1)S(1)} async-done(((bf16[8,64,512]{2,1,0:T(8,128)(2,1)}), bf16[8,64,512]{2,1,0:T(8,128)(2,1)S(1)}, u32[]{:S(2)}, u32[]{:S(2)}) %all-to-all-start.1) | async-done | bytes 524320 | tf_op jit(solution)/shard_map/all_to_all | solution.py:55
  121.2 1.4 %convolution_multiply_fusion = f32[512,512]{1,0:T(8,128)} fusion(bf16[512,512]{1,0:T(8,128)(2,1)S(1)} %bitcast.23, s32[512]{0:T(512)S(1)} %eq.48), kind=kOutput, calls=%fused_computation.4 | convolution fusion | flops 268959744 | bytes 1574912 | tf_op jit(solution)/shard_map/dot_general | solution.py:62
  (15 shorter events, 0.1 us)
Async XLA Ops:
  7.2 1.5 %copy-start.2 = (s32[256]{0:T(256)S(1)}, s32[256]{0:T(256)}, u32[]{:S(2)}) copy-start(s32[256]{0:T(256)} %param.9) | copy-start | bytes 3076
  7.2 64.8 %all-reduce.2.cloned.1.call-start = ((), (), s32[]{:S(2)}) async-start(), calls=%async_computation.2 | async-start | bytes 786432 | tf_op jit(solution)/shard_map/psum | solution.py:13
  10.3 43.7 %copy-start.1 = (bf16[96,768]{1,0:T(8,128)(2,1)S(1)}, bf16[96,768]{1,0:T(8,128)(2,1)}, u32[]{:S(2)}) copy-start(bf16[96,768]{1,0:T(8,128)(2,1)} %param.6) | copy-start | bytes 442372
  48.6 23.2 %copy-start = (bf16[256,768]{1,0:T(8,128)(2,1)S(1)}, bf16[256,768]{1,0:T(8,128)(2,1)}, u32[]{:S(2)}) copy-start(bf16[256,768]{1,0:T(8,128)(2,1)} %param.5) | copy-start | bytes 1179652
  48.6 58.9 %all-to-all-start = ((s32[8,1,64]{2,1,0:T(1,128)}), s32[8,1,64]{2,1,0:T(1,128)S(1)}, u32[]{:S(2)}, u32[]{:S(2)}) async-start(s32[8,1,64]{2,1,0:T(1,128)} %bitcast.8), calls=%async_computation | async-start | bytes 8192 | tf_op jit(solution)/shard_map/all_to_all | solution.py:56
  107.6 13.7 %all-to-all-start.1 = ((bf16[8,64,512]{2,1,0:T(8,128)(2,1)}), bf16[8,64,512]{2,1,0:T(8,128)(2,1)S(1)}, u32[]{:S(2)}, u32[]{:S(2)}) async-start(bf16[8,64,512]{2,1,0:T(8,128)(2,1)} %scatter_fusion.1), calls=%async_computation.1 | async-start | bytes 1048576 | tf_op jit(solution)/shard_map/all_to_all | solution.py:55
Sparse Core Ops, SparseCore 0:
  11.6 56.8 all-reduce.1
where the time goes:
time: 132 us; the launch traced here: 129 us
  local copies, waits for them, and re-layouts  73.6 us (56%)
  blocking collectives  17.6 us (13%)
  between operations  14.8 us (11%)
  starting transfers between devices  9.33 us (7%)
  waiting for transfers between devices  7.76 us (6%)
  other arithmetic  3.33 us (3%)
  matrix products  3.12 us (2%)
    scatter x1, local copies, waits for them, and re-layouts, body(): jnp.full((point_groups, capacity), -1, jnp.int32).at[owners, slot_rank]  38.3 us
    scatter x1, local copies, waits for them, and re-layouts, body(): slots = jnp.zeros((point_groups, capacity, features.shape[1]), jnp.bfloat...  33 us
    all_gather x1, blocking collectives, body(): lax.all_gather(landmarks, 'lmk', axis=0, tiled=True)  17.6 us
    all_to_all x1, waiting for transfers between devices, body(): lax.all_to_all(slots, 'pts', split_axis=0, concat_axis=0, tiled=True)  7.72 us
    all_to_all x1, starting transfers between devices, body(): lax.all_to_all(slot_ids, 'pts', split_axis=0, concat_axis=0, tiled=True)  5.37 us
    all_to_all x1, starting transfers between devices, body(): lax.all_to_all(slots, 'pts', split_axis=0, concat_axis=0, tiled=True)  3.92 us
  transfers between devices with their start and end apart: 3, of which 1 were waited for; matrix products, arithmetic and copies ran while one was open for 60% of the time, Pallas kernels for 0%

commit v1 on v0

v1 whole, which is shorter than its diff:
```python
import math

import jax
import jax.numpy as jnp
from jax import lax
from jax.experimental import pallas as pl
from jax.experimental.pallas import tpu as pltpu
from jax.sharding import PartitionSpec as P

CLUSTERS = 4096
LANES = 128
VMEM_LIMIT = 48 * 1024 * 1024
NT = (((1,), (1,)), ((), ()))


def unit_rows(values_in):
    widened = values_in.astype(jnp.float32)
    scale = lax.rsqrt(jnp.mean(widened * widened, axis=1, keepdims=True) + 1e-06)
    return (widened * scale).astype(jnp.bfloat16)


def rows_kernel(groups, capacity, points_ref, marks_ref, assignment_ref, out_ref):
    point_rows, marks = points_ref.shape[0], marks_ref.shape[0]
    owned = CLUSTERS // groups
    ids = assignment_ref[...]
    owners = lax.div(ids, owned)
    tags = ids - owners * owned + 1
    hits = lax.broadcasted_iota(jnp.int32, (groups, point_rows), 0) == owners
    earlier = lax.broadcasted_iota(jnp.int32, (point_rows, point_rows), 0) < lax.broadcasted_iota(
        jnp.int32, (point_rows, point_rows), 1
    )
    before = jnp.dot(
        hits.astype(jnp.float32).astype(jnp.bfloat16),
        earlier.astype(jnp.float32).astype(jnp.bfloat16),
        preferred_element_type=jnp.float32,
    )
    rank = jnp.sum(jnp.where(hits, before, 0.0), axis=0, keepdims=True).astype(jnp.int32)
    slots = owners * capacity + rank
    placed = (
        (lax.broadcasted_iota(jnp.int32, (groups * capacity, point_rows), 0) == slots)
        .astype(jnp.float32)
        .astype(jnp.bfloat16)
    )
    scores = lax.dot_general(
        unit_rows(points_ref[...]), unit_rows(marks_ref[...]), NT, preferred_element_type=jnp.float32
    )
    kernel = jnp.exp(scores * (0.5 / math.sqrt(points_ref.shape[1]))).astype(jnp.bfloat16)
    out_ref[:, :marks] = jnp.dot(placed, kernel, preferred_element_type=jnp.float32).astype(
        jnp.bfloat16
    )
    high = lax.div(tags, 256)
    which = lax.broadcasted_iota(jnp.int32, (LANES - marks, point_rows), 0)
    coded = jnp.where(which == 0, high, jnp.where(which == 1, tags - high * 256, 0))
    out_ref[:, marks:] = lax.dot_general(
        placed,
        coded.astype(jnp.float32).astype(jnp.bfloat16),
        NT,
        preferred_element_type=jnp.float32,
    ).astype(jnp.bfloat16)


def sums_kernel(scale, rows_ref, panel_ref, totals_ref, counts_ref):
    parts, slots, lanes = rows_ref.shape
    marks = panel_ref.shape[0] // parts
    owned = totals_ref.shape[0]
    features = jnp.dot(
        rows_ref[0, :, :marks], panel_ref[:marks, :], preferred_element_type=jnp.float32
    )
    for part in range(1, parts):
        features += jnp.dot(
            rows_ref[part, :, :marks],
            panel_ref[part * marks : (part + 1) * marks, :],
            preferred_element_type=jnp.float32,
        )
    features = features.astype(jnp.bfloat16)
    which = lax.broadcasted_iota(jnp.int32, (8, lanes - marks), 1)
    weights = jnp.where(which == 0, 256.0, jnp.where(which == 1, 1.0, 0.0)).astype(jnp.bfloat16)
    tags = lax.dot_general(
        weights, rows_ref[0, :, marks:], NT, preferred_element_type=jnp.float32
    )[:1].astype(jnp.int32)
    member = (
        (lax.broadcasted_iota(jnp.int32, (owned, slots), 0) + 1 == tags)
        .astype(jnp.float32)
        .astype(jnp.bfloat16)
    )
    totals_ref[...] = jnp.dot(member, features, preferred_element_type=jnp.float32) * scale
    counts_ref[...] = lax.dot_general(
        jnp.ones((8, slots), jnp.bfloat16), member, NT, preferred_element_type=jnp.float32
    )[:1].astype(jnp.int32)


def call(kernel, shapes, *operands):
    whole = pl.BlockSpec(memory_space=pltpu.VMEM)
    many = isinstance(shapes, tuple)
    return pl.pallas_call(
        kernel,
        out_shape=shapes,
        in_specs=[whole] * len(operands),
        out_specs=(whole,) * len(shapes) if many else whole,
        compiler_params=pltpu.CompilerParams(vmem_limit_bytes=VMEM_LIMIT),
    )(*operands)


def gather(block, axis):
    size = lax.axis_size(axis)
    return lax.all_to_all(
        jnp.broadcast_to(block[None], (size,) + block.shape), axis, split_axis=0, concat_axis=0, tiled=True
    )


def body(points, landmarks, panels, panel_index, assignment):
    groups = lax.axis_size("pts")
    point_rows = points.shape[0]
    capacity = 2 * point_rows // groups
    owned = CLUSTERS // groups
    depth, columns = panels.shape[1:]
    chunks = lax.all_to_all(
        panels.reshape(groups, depth // groups, columns), "pts", split_axis=0, concat_axis=0, tiled=True
    )
    chunk = lax.dynamic_index_in_dim(chunks, panel_index[0], 0, keepdims=False)
    panel = gather(chunk, "pts").reshape(depth, columns)
    rows = call(
        lambda *refs: rows_kernel(groups, capacity, *refs),
        jax.ShapeDtypeStruct((groups * capacity, LANES), jnp.bfloat16),
        points,
        landmarks,
        assignment.reshape(1, point_rows),
    )
    arrived = lax.all_to_all(
        rows.reshape(groups, capacity, LANES), "pts", split_axis=0, concat_axis=0, tiled=True
    ).reshape(groups * capacity, LANES)
    totals, counts = call(
        lambda *refs: sums_kernel(CLUSTERS / (point_rows * groups), *refs),
        (
            jax.ShapeDtypeStruct((owned, columns), jnp.float32),
            jax.ShapeDtypeStruct((1, owned), jnp.int32),
        ),
        gather(arrived, "lmk"),
        panel,
    )
    return (totals, counts.reshape(owned))


def solution(mesh):
    in_specs = (P("pts", None), P("lmk", None), P("pts", None, "lmk"), P(), P("pts"))
    out_specs = (P("pts", "lmk"), P("pts"))
    return jax.shard_map(body, mesh=mesh, in_specs=in_specs, out_specs=out_specs, check_vma=False)
```

time: 132 us -> 55.4 us (0.42); the launches traced: 129 us -> 55 us
  local copies, waits for them, and re-layouts: 73.6 us -> 0.77 us
  between operations: 14.8 us -> 1.35 us
  blocking collectives: 17.6 us -> 29.7 us
  Pallas kernels: 0 us -> 3.61 us
  other arithmetic: 3.33 us -> 0 us
  waiting for transfers between devices: 7.76 us -> 10.9 us
  matrix products: 3.12 us -> 0 us
    scatter x2 -> x0, local copies, waits for them, and re-layouts: 71.3 us -> none  [the longest x1 38.3 us: body(): jnp.full((point_groups, capacity), -1, jnp.int32).at[owners, slot_rank]]
    all_to_all x0 -> x2, blocking collectives: none -> 29.7 us  [gather(): lax.all_to_all(jnp.broadcast_to(block[None], (size,) + block.shape), axis...]
    all_gather x1 -> x0, blocking collectives: 17.6 us -> none  [body(): lax.all_gather(landmarks, 'lmk', axis=0, tiled=True)]
    pallas_call x0 -> x2, Pallas kernels: none -> 3.61 us  [call(): pl.pallas_call(kernel, out_shape=shapes, in_specs=[whole] * len(operands)...]
    all_to_all x2, waiting for transfers between devices: 7.73 us -> 10.9 us  [the longest x1 6.13 us: body(): lax.all_to_all(panels.reshape(groups, depth // groups, columns), 'pts', s...]
    dot_general x2 -> x0, matrix products: 3.12 us -> none  [the longest x1 1.7 us: body(): jnp.dot(kernel, factor_panel, preferred_element_type=jnp.float32)]
  transfers between devices with their start and end apart: 3 -> 2, of which waited for: 1 -> 2; matrix products, arithmetic and copies ran while one was open for 60% -> 0% of each run, Pallas kernels for 0% -> 3%
where the time goes in v1:
time: 55.4 us; the launch traced here: 55 us
  blocking collectives  29.7 us (54%)
  waiting for transfers between devices  10.9 us (20%)
  starting transfers between devices  8.69 us (16%)
  Pallas kernels  3.61 us (7%)
  between operations  1.35 us (2%)
  local copies, waits for them, and re-layouts  0.77 us (1%)
    all_to_all x2, blocking collectives, gather(): lax.all_to_all(jnp.broadcast_to(block[None], (size,) + block.shape), axis...  29.7 us
    all_to_all x1, waiting for transfers between devices, body(): lax.all_to_all(panels.reshape(groups, depth // groups, columns), 'pts', s...  6.13 us
    all_to_all x1, starting transfers between devices, body(): lax.all_to_all(panels.reshape(groups, depth // groups, columns), 'pts', s...  5.31 us
    all_to_all x1, waiting for transfers between devices, body(): lax.all_to_all(rows.reshape(groups, capacity, LANES), 'pts', split_axis=0...  4.79 us
    pallas_call x2, Pallas kernels, call(): pl.pallas_call(kernel, out_shape=shapes, in_specs=[whole] * len(operands)...  3.61 us
    all_to_all x1, starting transfers between devices, body(): lax.all_to_all(rows.reshape(groups, capacity, LANES), 'pts', split_axis=0...  3.37 us
  transfers between devices with their start and end apart: 2, of which 2 were waited for; matrix products, arithmetic and copies ran while one was open for 0% of the time, Pallas kernels for 3%

profile of v1, /device:TPU:0, one launch (start us, length us, event | category | flops | bytes accessed | tf_op | source)
XLA Modules:
  0.0 55.0 jit_solution(13700340442968149425)
XLA Ops:
  0.6 0.0 copy-start
  0.6 0.0 copy-start.1
  0.6 5.3 %all-to-all-start.2 = ((bf16[8,48,512]{2,1,0:T(8,128)(2,1)}), bf16[8,48,512]{2,1,0:T(8,128)(2,1)S(1)}, u32[]{:S(2)}, u32[]{:S(2)}) async-start(bf16[8,48,512]{2,1,0:T(8,128)(2,1)} %bitcast.15), calls=%async_computation.2 | async-start | bytes 786432 | tf_op jit(solution)/shard_map/all_to_all | solution.py:117
  6.0 0.0 copy-start.2
  6.0 0.0 copy-done
  6.0 0.0 copy-done.1
  6.0 0.7 %copy-done.2 = s32[256]{0:T(256)S(1)} copy-done((s32[256]{0:T(256)S(1)}, s32[256]{0:T(256)}, u32[]{:S(2)}) %copy-start.2) | copy-done | bytes 1048
  6.6 1.5 %shard_map.68 = bf16[512,128]{1,0:T(8,128)(2,1)} custom-call(bf16[256,768]{1,0:T(8,128)(2,1)S(1)} %copy-done, bf16[96,768]{1,0:T(8,128)(2,1)S(1)} %copy-done.1, s32[1,256]{1,0:T(1,128)S(1)} %bitcast.13), custom_call_target="tpu_custom_call" | custom-call | tf_op jit(solution)/shard_map/pallas_call | solution.py:95
  8.2 6.1 %all-to-all-done.2 = bf16[8,48,512]{2,1,0:T(8,128)(2,1)S(1)} async-done(((bf16[8,48,512]{2,1,0:T(8,128)(2,1)}), bf16[8,48,512]{2,1,0:T(8,128)(2,1)S(1)}, u32[]{:S(2)}, u32[]{:S(2)}) %all-to-all-start.2) | async-done | bytes 393248 | tf_op jit(solution)/shard_map/all_to_all | solution.py:117
  14.3 3.4 %all-to-all-start = ((bf16[8,64,128]{2,1,0:T(8,128)(2,1)}), bf16[8,64,128]{2,1,0:T(8,128)(2,1)S(1)}, u32[]{:S(2)}, u32[]{:S(2)}) async-start(bf16[8,64,128]{2,1,0:T(8,128)(2,1)} %bitcast.1), calls=%async_computation | async-start | bytes 262144 | tf_op jit(solution)/shard_map/all_to_all | solution.py:129
  18.4 4.8 %all-to-all-done = bf16[8,64,128]{2,1,0:T(8,128)(2,1)S(1)} async-done(((bf16[8,64,128]{2,1,0:T(8,128)(2,1)}), bf16[8,64,128]{2,1,0:T(8,128)(2,1)S(1)}, u32[]{:S(2)}, u32[]{:S(2)}) %all-to-all-start) | async-done | bytes 131104 | tf_op jit(solution)/shard_map/all_to_all | solution.py:129
  23.2 10.7 %all_to_all.20 = bf16[8,48,512]{2,1,0:T(8,128)(2,1)S(1)} all-to-all(bf16[8,48,512]{2,1,0:T(8,128)(2,1)S(1)} %broadcast_in_dim.18), channel_id=1, replica_groups=mesh['pts'=8,'lmk'=4] {'pts'}, dimensions={0} | all-to-all | bytes 786432 | tf_op jit(solution)/shard_map/all_to_all | solution.py:106
  33.9 0.1 broadcast_in_dim.16
  34.0 19.0 %all_to_all.21.refs_0_ = bf16[4,512,128]{2,1,0:T(8,128)(2,1)S(1)} all-to-all(bf16[4,512,128]{2,1,0:T(8,128)(2,1)S(1)} %broadcast_in_dim.16), channel_id=1, replica_groups=mesh['pts'=8,'lmk'=4] {'lmk'}, dimensions={0} | all-to-all | bytes 1048576 | tf_op jit(solution)/shard_map/all_to_all | solution.py:106
  53.0 2.1 %shard_map.69 = (f32[512,512]{1,0:T(8,128)}, s32[1,512]{1,0:T(1,128)}) custom-call(bf16[4,512,128]{2,1,0:T(8,128)(2,1)S(1)} %all_to_all.21.refs_0_, bf16[384,512]{1,0:T(8,128)(2,1)S(1)} %bitcast.12), custom_call_target="tpu_custom_call" | custom-call | tf_op jit(solution)/shard_map/pallas_call | solution.py:95
  (2 shorter events, 0.0 us)
Async XLA Ops:
  0.6 5.3 %copy-start = (bf16[256,768]{1,0:T(8,128)(2,1)S(1)}, bf16[256,768]{1,0:T(8,128)(2,1)}, u32[]{:S(2)}) copy-start(bf16[256,768]{1,0:T(8,128)(2,1)} %refs_0_.1) | copy-start | bytes 1179652
  0.6 5.3 %copy-start.1 = (bf16[96,768]{1,0:T(8,128)(2,1)S(1)}, bf16[96,768]{1,0:T(8,128)(2,1)}, u32[]{:S(2)}) copy-start(bf16[96,768]{1,0:T(8,128)(2,1)} %refs_1_.1) | copy-start | bytes 442372
  0.6 13.7 %all-to-all-start.2 = ((bf16[8,48,512]{2,1,0:T(8,128)(2,1)}), bf16[8,48,512]{2,1,0:T(8,128)(2,1)S(1)}, u32[]{:S(2)}, u32[]{:S(2)}) async-start(bf16[8,48,512]{2,1,0:T(8,128)(2,1)} %bitcast.15), calls=%async_computation.2 | async-start | bytes 786432 | tf_op jit(solution)/shard_map/all_to_all | solution.py:117
  6.0 0.7 %copy-start.2 = (s32[256]{0:T(256)S(1)}, s32[256]{0:T(256)}, u32[]{:S(2)}) copy-start(s32[256]{0:T(256)} %param.9) | copy-start | bytes 3076
  14.3 8.8 %all-to-all-start = ((bf16[8,64,128]{2,1,0:T(8,128)(2,1)}), bf16[8,64,128]{2,1,0:T(8,128)(2,1)S(1)}, u32[]{:S(2)}, u32[]{:S(2)}) async-start(bf16[8,64,128]{2,1,0:T(8,128)(2,1)} %bitcast.1), calls=%async_computation | async-start | bytes 262144 | tf_op jit(solution)/shard_map/all_to_all | solution.py:129

commit v2 on v1

v2 whole, which is shorter than its diff:
```python
import math

import jax
import jax.numpy as jnp
from jax import lax
from jax.experimental import pallas as pl
from jax.experimental.pallas import tpu as pltpu
from jax.sharding import PartitionSpec as P

CLUSTERS = 4096
LANES = 128
VMEM_LIMIT = 48 * 1024 * 1024
NT = (((1,), (1,)), ((), ()))


def unit_rows(values_in):
    widened = values_in.astype(jnp.float32)
    scale = lax.rsqrt(jnp.mean(widened * widened, axis=1, keepdims=True) + 1e-06)
    return (widened * scale).astype(jnp.bfloat16)


def rows_kernel(groups, capacity, *refs):
    place_ref, points_ref, own_ref, assignment_ref = refs[:4]
    halves, out_ref, marks_ref = refs[4:-2], refs[-2], refs[-1]
    point_rows = points_ref.shape[0]
    own, all_marks = own_ref.shape[0], marks_ref.shape[0]
    half = own // 2
    parity = lax.rem(place_ref[0], 2)
    ids = assignment_ref[...]
    owned = CLUSTERS // groups
    owners = lax.div(ids, owned)
    tags = ids - owners * owned + 1
    hits = lax.broadcasted_iota(jnp.int32, (groups, point_rows), 0) == owners
    earlier = lax.broadcasted_iota(jnp.int32, (point_rows, point_rows), 0) < lax.broadcasted_iota(
        jnp.int32, (point_rows, point_rows), 1
    )
    before = jnp.dot(
        hits.astype(jnp.float32).astype(jnp.bfloat16),
        earlier.astype(jnp.float32).astype(jnp.bfloat16),
        preferred_element_type=jnp.float32,
    )
    rank = jnp.sum(jnp.where(hits, before, 0.0), axis=0, keepdims=True).astype(jnp.int32)
    slots = owners * capacity + rank
    placed = (
        (lax.broadcasted_iota(jnp.int32, (groups * capacity, point_rows), 0) == slots)
        .astype(jnp.float32)
        .astype(jnp.bfloat16)
    )
    marks_ref[:own, :] = unit_rows(own_ref[...])
    for at, (mine, other) in enumerate(zip(halves[::2], halves[1::2])):
        first = own * (at + 1)
        marks_ref[pl.ds(pl.multiple_of(first + half * parity, 16), half), :] = unit_rows(mine[...])
        marks_ref[pl.ds(pl.multiple_of(first + half * (1 - parity), 16), half), :] = unit_rows(
            other[...]
        )
    scores = lax.dot_general(
        unit_rows(points_ref[...]), marks_ref[...], NT, preferred_element_type=jnp.float32
    )
    kernel = jnp.exp(scores * (0.5 / math.sqrt(points_ref.shape[1]))).astype(jnp.bfloat16)
    out_ref[:, :all_marks] = jnp.dot(placed, kernel, preferred_element_type=jnp.float32).astype(
        jnp.bfloat16
    )
    high = lax.div(tags, 256)
    which = lax.broadcasted_iota(jnp.int32, (LANES, point_rows), 0)
    coded = jnp.where(which == 0, high, jnp.where(which == 1, tags - high * 256, 0))
    out_ref[:, all_marks:] = lax.dot_general(
        placed,
        coded.astype(jnp.float32).astype(jnp.bfloat16),
        NT,
        preferred_element_type=jnp.float32,
    ).astype(jnp.bfloat16)


def sums_kernel(scale, parts, place_ref, rows_ref, panel_ref, totals_ref, counts_ref, turned_ref):
    slots = rows_ref.shape[0]
    depth = panel_ref.shape[0]
    owned, own = totals_ref.shape[0], depth // parts
    for part in range(parts):
        source = lax.rem(place_ref[1] + parts - part, parts)
        turned_ref[part * own : (part + 1) * own, :] = panel_ref[
            pl.ds(pl.multiple_of(source * own, 16), own), :
        ]
    features = jnp.dot(
        rows_ref[:, :depth], turned_ref[...], preferred_element_type=jnp.float32
    ).astype(jnp.bfloat16)
    which = lax.broadcasted_iota(jnp.int32, (8, LANES), 1)
    weights = jnp.where(which == 0, 256.0, jnp.where(which == 1, 1.0, 0.0)).astype(jnp.bfloat16)
    tags = lax.dot_general(
        weights, rows_ref[:, depth:], NT, preferred_element_type=jnp.float32
    )[:1].astype(jnp.int32)
    member = (
        (lax.broadcasted_iota(jnp.int32, (owned, slots), 0) + 1 == tags)
        .astype(jnp.float32)
        .astype(jnp.bfloat16)
    )
    totals_ref[...] = jnp.dot(member, features, preferred_element_type=jnp.float32) * scale
    counts_ref[...] = lax.dot_general(
        jnp.ones((8, slots), jnp.bfloat16), member, NT, preferred_element_type=jnp.float32
    )[:1].astype(jnp.int32)


def call(kernel, shapes, scratch, place, *operands):
    whole = pl.BlockSpec(memory_space=pltpu.VMEM)
    many = isinstance(shapes, tuple)
    return pl.pallas_call(
        kernel,
        out_shape=shapes,
        in_specs=[pl.BlockSpec(memory_space=pltpu.SMEM)] + [whole] * len(operands),
        out_specs=(whole,) * len(shapes) if many else whole,
        scratch_shapes=[scratch],
        compiler_params=pltpu.CompilerParams(vmem_limit_bytes=VMEM_LIMIT),
    )(place, *operands)


def gather(block, axis):
    size = lax.axis_size(axis)
    return lax.all_to_all(
        jnp.broadcast_to(block[None], (size,) + block.shape), axis, split_axis=0, concat_axis=0, tiled=True
    )


def shift(block, axis, by):
    size = lax.axis_size(axis)
    return lax.ppermute(block, axis, [(i, (i + by) % size) for i in range(size)])


def swap(block, axis):
    return lax.ppermute(block, axis, [(i, i ^ 1) for i in range(lax.axis_size(axis))])


def body(points, landmarks, panels, panel_index, assignment):
    groups, parts = lax.axis_size("pts"), lax.axis_size("lmk")
    point_rows = points.shape[0]
    capacity = 2 * point_rows // groups
    owned = CLUSTERS // groups
    depth, columns = panels.shape[1:]
    own, width = landmarks.shape
    place = jnp.stack([lax.axis_index("pts"), lax.axis_index("lmk")]).astype(jnp.int32)
    mine = lax.dynamic_slice_in_dim(landmarks, (place[0] % 2) * (own // 2), own // 2, 0)
    halves = []
    for by in range(1, parts):
        half = shift(mine, "lmk", by)
        halves += [half, swap(half, "pts")]
    chunks = lax.all_to_all(
        panels.reshape(groups, depth // groups, columns), "pts", split_axis=0, concat_axis=0, tiled=True
    )
    chunk = lax.dynamic_index_in_dim(chunks, panel_index[0], 0, keepdims=False)
    panel = gather(chunk, "pts").reshape(depth, columns)
    row_lanes = depth + LANES
    rows = call(
        lambda *refs: rows_kernel(groups, capacity, *refs),
        jax.ShapeDtypeStruct((groups * capacity, row_lanes), jnp.bfloat16),
        pltpu.VMEM((depth, width), jnp.bfloat16),
        place,
        points,
        landmarks,
        assignment.reshape(1, point_rows),
        *halves,
    )
    arrived = lax.all_to_all(
        rows.reshape(groups, capacity, row_lanes), "pts", split_axis=0, concat_axis=0, tiled=True
    ).reshape(groups * capacity, row_lanes)
    totals, counts = call(
        lambda *refs: sums_kernel(CLUSTERS / (point_rows * groups), parts, *refs),
        (
            jax.ShapeDtypeStruct((owned, columns), jnp.float32),
            jax.ShapeDtypeStruct((1, owned), jnp.int32),
        ),
        pltpu.VMEM((depth, columns), jnp.bfloat16),
        place,
        arrived,
        panel,
    )
    return (totals, counts.reshape(owned))


def solution(mesh):
    in_specs = (P("pts", None), P("lmk", None), P("pts", None, "lmk"), P(), P("pts"))
    out_specs = (P("pts", "lmk"), P("pts"))
    return jax.shard_map(body, mesh=mesh, in_specs=in_specs, out_specs=out_specs, check_vma=False)
```

time: 55.4 us -> 48.3 us (0.87)
  blocking collectives: 29.7 us -> 10.7 us
  waiting for transfers between devices: 10.9 us -> 16.7 us
  starting transfers between devices: 8.69 us -> 14.3 us
  Pallas kernels: 3.61 us -> 4.74 us
  local copies, waits for them, and re-layouts: 0.77 us -> 0.06 us
    all_to_all x2 -> x1, blocking collectives: 29.7 us -> 10.7 us  [gather(): lax.all_to_all(jnp.broadcast_to(block[None], (size,) + block.shape), axis...]
    ppermute x0 -> x6, waiting for transfers between devices: none -> 7.65 us  [the longest x3 6.81 us: shift(): lax.ppermute(block, axis, [(i, (i + by) % size) for i in range(size)])]
    all_to_all x1, waiting for transfers between devices: 6.13 us -> 0.01 us  [body(): lax.all_to_all(panels.reshape(groups, depth // groups, columns), 'pts', s...]
    ppermute x0 -> x6, starting transfers between devices: none -> 5.18 us  [the longest x3 4.67 us: shift(): lax.ppermute(block, axis, [(i, (i + by) % size) for i in range(size)])]
    all_to_all x1, waiting for transfers between devices: 4.79 us -> 9.07 us  [body(): lax.all_to_all(rows.reshape(groups, capacity, row_lanes), 'pts', split_ax...]
    pallas_call x2, Pallas kernels: 3.61 us -> 4.74 us  [call(): pl.pallas_call(kernel, out_shape=shapes, in_specs=[pl.BlockSpec(memory_sp...]
    unnamed x6, local copies, waits for them, and re-layouts: 0.66 us -> 0.01 us
  transfers between devices with their start and end apart: 2 -> 8, of which waited for: 2 -> 5; matrix products, arithmetic and copies ran while one was open for 0% -> 0% of each run, Pallas kernels for 3% -> 5%
where the time goes in v2:
time: 48.3 us; the launch traced here: 47.9 us
  waiting for transfers between devices  16.7 us (35%)
  starting transfers between devices  14.3 us (30%)
  blocking collectives  10.7 us (22%)
  Pallas kernels  4.74 us (10%)
  between operations  1.34 us (3%)
    all_to_all x1, blocking collectives, gather(): lax.all_to_all(jnp.broadcast_to(block[None], (size,) + block.shape), axis...  10.7 us
    all_to_all x1, waiting for transfers between devices, body(): lax.all_to_all(rows.reshape(groups, capacity, row_lanes), 'pts', split_ax...  9.07 us
    ppermute x3, waiting for transfers between devices, shift(): lax.ppermute(block, axis, [(i, (i + by) % size) for i in range(size)])  6.81 us
    all_to_all x1, starting transfers between devices, body(): lax.all_to_all(panels.reshape(groups, depth // groups, columns), 'pts', s...  5.31 us
    pallas_call x2, Pallas kernels, call(): pl.pallas_call(kernel, out_shape=shapes, in_specs=[pl.BlockSpec(memory_sp...  4.74 us
    ppermute x3, starting transfers between devices, shift(): lax.ppermute(block, axis, [(i, (i + by) % size) for i in range(size)])  4.67 us
    all_to_all x1, starting transfers between devices, body(): lax.all_to_all(rows.reshape(groups, capacity, row_lanes), 'pts', split_ax...  3.77 us
  transfers between devices with their start and end apart: 8, of which 5 were waited for; matrix products, arithmetic and copies ran while one was open for 0% of the time, Pallas kernels for 5%

profile of v2, /device:TPU:0, one launch (start us, length us, event | category | flops | bytes accessed | tf_op | source)
XLA Modules:
  0.0 47.9 jit_solution(2004585879542940710)
XLA Ops:
  0.6 0.0 copy-start.1
  0.6 0.0 copy-start
  0.6 5.3 %all-to-all-start.1 = ((bf16[8,48,512]{2,1,0:T(8,128)(2,1)}), bf16[8,48,512]{2,1,0:T(8,128)(2,1)S(1)}, u32[]{:S(2)}, u32[]{:S(2)}) async-start(bf16[8,48,512]{2,1,0:T(8,128)(2,1)} %bitcast.17), calls=%async_computation.1 | async-start | bytes 786432 | tf_op jit(solution)/shard_map/all_to_all | solution.py:144
  6.0 0.0 copy-done.1
  6.0 3.7 %collective-permute-start.4 = (bf16[48,768]{1,0:T(8,128)(2,1)S(1)}, bf16[48,768]{1,0:T(8,128)(2,1)S(1)}, u32[]{:S(2)}, u32[]{:S(2)}) collective-permute-start(bf16[48,768]{1,0:T(8,128)(2,1)S(1)} %constant_dynamic-slice_fusion), channel_id=1, source_target_pairs={{0,3},{1,0},{2,1},{3,2},{4,7},{5,4},{6,5},{7,6},{8,11},{9,8},{10,9... | collective-permute-start | bytes 221192 | tf_op jit(solution)/shard_map/ppermute | solution.py:124
  9.6 0.0 collective-permute-start.2
  9.6 1.0 %collective-permute-start = (bf16[48,768]{1,0:T(8,128)(2,1)S(1)}, bf16[48,768]{1,0:T(8,128)(2,1)S(1)}, u32[]{:S(2)}, u32[]{:S(2)}) collective-permute-start(bf16[48,768]{1,0:T(8,128)(2,1)S(1)} %constant_dynamic-slice_fusion), channel_id=1, source_target_pairs={{0,1},{1,2},{2,3},{3,0},{4,5},{5,6},{6,7},{7,4},{8,9},{9,10},{10,1... | collective-permute-start | bytes 221192 | tf_op jit(solution)/shard_map/ppermute | solution.py:124
  10.7 1.6 %collective-permute-done.4.refs_8_ = bf16[48,768]{1,0:T(8,128)(2,1)S(1)} collective-permute-done((bf16[48,768]{1,0:T(8,128)(2,1)S(1)}, bf16[48,768]{1,0:T(8,128)(2,1)S(1)}, u32[]{:S(2)}, u32[]{:S(2)}) %collective-permute-start.4) | collective-permute-done | bytes 73760 | tf_op jit(solution)/shard_map/ppermute | solution.py:124
  12.3 0.0 collective-permute-start.5
  12.3 5.2 %collective-permute-done.2.refs_6_ = bf16[48,768]{1,0:T(8,128)(2,1)S(1)} collective-permute-done((bf16[48,768]{1,0:T(8,128)(2,1)S(1)}, bf16[48,768]{1,0:T(8,128)(2,1)S(1)}, u32[]{:S(2)}, u32[]{:S(2)}) %collective-permute-start.2) | collective-permute-done | bytes 73760 | tf_op jit(solution)/shard_map/ppermute | solution.py:124
  17.5 0.0 collective-permute-start.3
  17.5 0.0 collective-permute-done.refs_4_
  17.5 0.5 collective-permute-start.1
  18.0 0.1 pad_add_fusion.refs_0_
  18.1 0.0 collective-permute-done.5.refs_9_
  18.1 0.7 %collective-permute-done.3.refs_7_ = bf16[48,768]{1,0:T(8,128)(2,1)S(1)} collective-permute-done((bf16[48,768]{1,0:T(8,128)(2,1)S(1)}, bf16[48,768]{1,0:T(8,128)(2,1)S(1)}, u32[]{:S(2)}, u32[]{:S(2)}) %collective-permute-start.3) | collective-permute-done | bytes 73760 | tf_op jit(solution)/shard_map/ppermute | solution.py:128
  18.7 0.2 collective-permute-done.1.refs_5_
  18.9 0.0 copy-done
  18.9 2.4 %shard_map.68 = bf16[512,512]{1,0:T(8,128)(2,1)} custom-call(s32[2]{0:T(128)S(1)} %pad_add_fusion.refs_0_, bf16[256,768]{1,0:T(8,128)(2,1)S(1)} %copy-done, bf16[96,768]{1,0:T(8,128)(2,1)S(1)} %copy-done.1, s32[1,256]{1,0:T(1,128)S(1)} %bitcast.16, bf16[48,768]{1,0:T(8,128)(2,1)S(1)} %collective-permute-done.refs_4_, ...), custom_call_target="tpu_custom_call" | custom-call | tf_op jit(solution)/shard_map/pallas_call | solution.py:105
  21.3 0.0 all-to-all-done.1
  21.3 3.8 %all-to-all-start = ((bf16[8,64,512]{2,1,0:T(8,128)(2,1)}), bf16[8,64,512]{2,1,0:T(8,128)(2,1)S(1)}, u32[]{:S(2)}, u32[]{:S(2)}) async-start(bf16[8,64,512]{2,1,0:T(8,128)(2,1)} %bitcast.3), calls=%async_computation | async-start | bytes 1048576 | tf_op jit(solution)/shard_map/all_to_all | solution.py:160
  25.7 9.1 %all-to-all-done = bf16[8,64,512]{2,1,0:T(8,128)(2,1)S(1)} async-done(((bf16[8,64,512]{2,1,0:T(8,128)(2,1)}), bf16[8,64,512]{2,1,0:T(8,128)(2,1)S(1)}, u32[]{:S(2)}, u32[]{:S(2)}) %all-to-all-start) | async-done | bytes 524320 | tf_op jit(solution)/shard_map/all_to_all | solution.py:160
  34.8 10.7 %all_to_all.15 = bf16[8,48,512]{2,1,0:T(8,128)(2,1)S(1)} all-to-all(bf16[8,48,512]{2,1,0:T(8,128)(2,1)S(1)} %broadcast_in_dim.9), channel_id=1, replica_groups=mesh['pts'=8,'lmk'=4] {'pts'}, dimensions={0} | all-to-all | bytes 786432 | tf_op jit(solution)/shard_map/all_to_all | solution.py:117
  45.6 2.4 %shard_map.69 = (f32[512,512]{1,0:T(8,128)}, s32[1,512]{1,0:T(1,128)}) custom-call(s32[2]{0:T(128)S(1)} %pad_add_fusion.refs_0_, bf16[512,512]{1,0:T(8,128)(2,1)S(1)} %bitcast.14, bf16[384,512]{1,0:T(8,128)(2,1)S(1)} %bitcast.15), custom_call_target="tpu_custom_call" | custom-call | tf_op jit(solution)/shard_map/pallas_call | solution.py:105
  (5 shorter events, 0.1 us)
Async XLA Ops:
  0.6 5.3 %copy-start.1 = (bf16[96,768]{1,0:T(8,128)(2,1)S(1)}, bf16[96,768]{1,0:T(8,128)(2,1)}, u32[]{:S(2)}) copy-start(bf16[96,768]{1,0:T(8,128)(2,1)} %refs_2_.1) | copy-start | bytes 442372
  0.6 18.3 %copy-start = (bf16[256,768]{1,0:T(8,128)(2,1)S(1)}, bf16[256,768]{1,0:T(8,128)(2,1)}, u32[]{:S(2)}) copy-start(bf16[256,768]{1,0:T(8,128)(2,1)} %refs_1_.1) | copy-start | bytes 1179652
  0.6 20.6 %all-to-all-start.1 = ((bf16[8,48,512]{2,1,0:T(8,128)(2,1)}), bf16[8,48,512]{2,1,0:T(8,128)(2,1)S(1)}, u32[]{:S(2)}, u32[]{:S(2)}) async-start(bf16[8,48,512]{2,1,0:T(8,128)(2,1)} %bitcast.17), calls=%async_computation.1 | async-start | bytes 786432 | tf_op jit(solution)/shard_map/all_to_all | solution.py:144
  6.0 6.3 %collective-permute-start.4 = (bf16[48,768]{1,0:T(8,128)(2,1)S(1)}, bf16[48,768]{1,0:T(8,128)(2,1)S(1)}, u32[]{:S(2)}, u32[]{:S(2)}) collective-permute-start(bf16[48,768]{1,0:T(8,128)(2,1)S(1)} %constant_dynamic-slice_fusion), channel_id=1, source_target_pairs={{0,3},{1,0},{2,1},{3,2},{4,7},{5,4},{6,5},{7,6},{8,11},{9,8},{10,9... | collective-permute-start | bytes 221192 | tf_op jit(solution)/shard_map/ppermute | solution.py:124
  9.6 7.8 %collective-permute-start.2 = (bf16[48,768]{1,0:T(8,128)(2,1)S(1)}, bf16[48,768]{1,0:T(8,128)(2,1)S(1)}, u32[]{:S(2)}, u32[]{:S(2)}) collective-permute-start(bf16[48,768]{1,0:T(8,128)(2,1)S(1)} %constant_dynamic-slice_fusion), channel_id=1, source_target_pairs={{0,2},{1,3},{2,0},{3,1},{4,6},{5,7},{6,4},{7,5},{8,10},{9,11},{10,... | collective-permute-start | bytes 221192 | tf_op jit(solution)/shard_map/ppermute | solution.py:124
  9.6 7.9 %collective-permute-start = (bf16[48,768]{1,0:T(8,128)(2,1)S(1)}, bf16[48,768]{1,0:T(8,128)(2,1)S(1)}, u32[]{:S(2)}, u32[]{:S(2)}) collective-permute-start(bf16[48,768]{1,0:T(8,128)(2,1)S(1)} %constant_dynamic-slice_fusion), channel_id=1, source_target_pairs={{0,1},{1,2},{2,3},{3,0},{4,5},{5,6},{6,7},{7,4},{8,9},{9,10},{10,1... | collective-permute-start | bytes 221192 | tf_op jit(solution)/shard_map/ppermute | solution.py:124
  12.3 5.8 %collective-permute-start.5 = (bf16[48,768]{1,0:T(8,128)(2,1)S(1)}, bf16[48,768]{1,0:T(8,128)(2,1)S(1)}, u32[]{:S(2)}, u32[]{:S(2)}) collective-permute-start(bf16[48,768]{1,0:T(8,128)(2,1)S(1)} %collective-permute-done.4.refs_8_), channel_id=1, source_target_pairs={{0,4},{4,0},{8,12},{12,8},{16,20},{20,16},{24,28},{28,24},{1,5},{5... | collective-permute-start | bytes 221192 | tf_op jit(solution)/shard_map/ppermute | solution.py:128
  17.5 1.3 %collective-permute-start.3 = (bf16[48,768]{1,0:T(8,128)(2,1)S(1)}, bf16[48,768]{1,0:T(8,128)(2,1)S(1)}, u32[]{:S(2)}, u32[]{:S(2)}) collective-permute-start(bf16[48,768]{1,0:T(8,128)(2,1)S(1)} %collective-permute-done.2.refs_6_), channel_id=1, source_target_pairs={{0,4},{4,0},{8,12},{12,8},{16,20},{20,16},{24,28},{28,24},{1,5},{5... | collective-permute-start | bytes 221192 | tf_op jit(solution)/shard_map/ppermute | solution.py:128
  17.5 1.4 %collective-permute-start.1 = (bf16[48,768]{1,0:T(8,128)(2,1)S(1)}, bf16[48,768]{1,0:T(8,128)(2,1)S(1)}, u32[]{:S(2)}, u32[]{:S(2)}) collective-permute-start(bf16[48,768]{1,0:T(8,128)(2,1)S(1)} %collective-permute-done.refs_4_), channel_id=1, source_target_pairs={{0,4},{4,0},{8,12},{12,8},{16,20},{20,16},{24,28},{28,24},{1,5},{5... | collective-permute-start | bytes 221192 | tf_op jit(solution)/shard_map/ppermute | solution.py:128
  18.1 0.8 %copy-start.2 = (s32[256]{0:T(256)S(1)}, s32[256]{0:T(256)}, u32[]{:S(2)}) copy-start(s32[256]{0:T(256)} %param.9) | copy-start | bytes 3076
  21.3 13.5 %all-to-all-start = ((bf16[8,64,512]{2,1,0:T(8,128)(2,1)}), bf16[8,64,512]{2,1,0:T(8,128)(2,1)S(1)}, u32[]{:S(2)}, u32[]{:S(2)}) async-start(bf16[8,64,512]{2,1,0:T(8,128)(2,1)} %bitcast.3), calls=%async_computation | async-start | bytes 1048576 | tf_op jit(solution)/shard_map/all_to_all | solution.py:160
